TPU v7x, 32 devices: a whole 2x2x4 slice. The times are simulated.
32 devices in a mesh: lon: 8 (over z, x), lat: 4 (over y, core).
Axes of the slice: x: 2, y: 2, z: 4, core: 2. Of those that a mesh axis runs over, the one named last changes fastest.
Arguments:
- misfit: float32 [16, 256, 2048], P(None, 'lat', 'lon'), may hold values from -6 to 6
- east_wind: bfloat16 [6, 16, 256, 2048], P(None, None, 'lat', 'lon'), may hold values from -0.24 to 0.24
- north_wind: bfloat16 [6, 16, 256, 2048], P(None, None, 'lat', 'lon'), may hold values from -0.24 to 0.24
- mixing: bfloat16 [15, 256, 2048], P(None, 'lat', 'lon'), may hold values from 0.019897461 to 0.23925781
- lon_corr: bfloat16 [2048, 2048], P('lon'), as said below
- lat_corr: bfloat16 [256, 256], P('lat'), as said below
Outputs:
- flux_gradient: float32 [256, 2048], P('lat', 'lon')
- adjoint_state: float32 [16, 256, 2048], P(None, 'lat', 'lon')
Inputs may be any that keep to these rules, and one draw needn't show every extreme that they name: lon_corr is exactly symmetric. lat_corr is exactly symmetric.
All inputs are finite; a program needn't handle non-finite values.
Results may differ from a plain program's by a relative error of at most 0.0041.
Values may be sent and summed in bfloat16 or wider, within the bound.
A program may use at most 128 MiB of HBM per device.

v0:
```python
import jax
import jax.numpy as jnp
from jax import lax
from jax.sharding import PartitionSpec as P


def with_halo(cells, sides, width):
    for axis, dim in sides:
        count = lax.axis_size(axis)
        head = lax.slice_in_dim(cells, 0, width, axis=dim)
        tail = lax.slice_in_dim(cells, cells.shape[dim] - width, cells.shape[dim], axis=dim)
        cells = jnp.concatenate(
            [
                lax.ppermute(tail, axis, [(i, (i + 1) % count) for i in range(count)]),
                cells,
                lax.ppermute(head, axis, [((i + 1) % count, i) for i in range(count)]),
            ],
            axis=dim,
        )
    return cells


def shifted(value, axis, steps):
    count = lax.axis_size(axis)
    pairs = [(source, (source + steps) % count) for source in range(count)]
    return lax.ppermute(value, axis, pairs)


def from_behind(shard, axis, by):
    length = lax.axis_size(axis)
    pairs = [(i, i + by) for i in range(length) if 0 <= i + by < length]
    return lax.ppermute(shard, axis, pairs)


def exchange_margin(field, depth):
    return with_halo(field, (("lon", 2), ("lat", 1)), depth)


def transport(
    adjoint,
    east_face,
    west_face,
    north_face,
    south_face,
    east_side,
    west_side,
    north_side,
    south_side,
    kappa,
):
    moved = (
        adjoint
        + jnp.maximum(east_face, 0.0) * (east_side - adjoint)
        + jnp.minimum(west_face, 0.0) * (adjoint - west_side)
        + jnp.maximum(north_face, 0.0) * (north_side - adjoint)
        + jnp.minimum(south_face, 0.0) * (adjoint - south_side)
    )
    flux = kappa * (moved[1:] - moved[:-1])
    return moved + jnp.pad(flux, ((0, 1), (0, 0), (0, 0))) - jnp.pad(flux, ((1, 0), (0, 0), (0, 0)))


def per_device(misfit, east_wind, north_wind, mixing, lon_corr, lat_corr):
    adjoint = misfit
    levels, lat_rows, lon_cols = adjoint.shape
    num_steps = east_wind.shape[0]
    kappa = mixing.astype(jnp.float32)
    grad = jnp.zeros((lat_rows, lon_cols), jnp.float32)
    last_band = lax.axis_index("lat") == lax.axis_size("lat") - 1
    row_ids = lax.broadcasted_iota(jnp.int32, (1, lat_rows, 1), 1)
    keep_north = jnp.logical_not(jnp.logical_and(last_band, row_ids == lat_rows - 1)).astype(
        jnp.float32
    )
    west_all = shifted(east_wind[:, :, :, -1:], "lon", 1)
    south_all = from_behind(north_wind[:, :, -1:, :], "lat", 1)
    for section in reversed(range(num_steps)):
        east_raw = east_wind[section]
        north_raw = north_wind[section]
        west_rim = west_all[section]
        south_rim = south_all[section]
        east_face = east_raw.astype(jnp.float32)
        west_face = jnp.concatenate([west_rim.astype(jnp.float32), east_face[:, :, :-1]], axis=2)
        north_face = north_raw.astype(jnp.float32) * keep_north
        south_face = jnp.concatenate([south_rim.astype(jnp.float32), north_face[:, :-1, :]], axis=1)
        padded = exchange_margin(adjoint, 1)
        adjoint = transport(
            adjoint,
            east_face,
            west_face,
            north_face,
            south_face,
            padded[:, 1:-1, 2:],
            padded[:, 1:-1, :-2],
            padded[:, 2:, 1:-1],
            padded[:, :-2, 1:-1],
            kappa,
        )
        grad = grad + adjoint[0]
    surface = (grad / num_steps).astype(jnp.bfloat16)
    block = lon_corr
    zonal = lax.dot_general(
        lax.all_gather(surface, "lon", axis=1, tiled=True),
        block,
        (((1,), (1,)), ((), ())),
        preferred_element_type=jnp.float32,
    ).astype(jnp.bfloat16)
    block = lat_corr
    flux_gradient = jnp.dot(
        block, lax.all_gather(zonal, "lat", axis=0, tiled=True), preferred_element_type=jnp.float32
    )
    return (flux_gradient, adjoint)


def solution(mesh):
    placed = (
        P(None, "lat", "lon"),
        P(None, None, "lat", "lon"),
        P(None, None, "lat", "lon"),
        P(None, "lat", "lon"),
        P("lon", None),
        P("lat", None),
    )
    return jax.shard_map(
        per_device,
        mesh=mesh,
        in_specs=placed,
        out_specs=(P("lat", "lon"), P(None, "lat", "lon")),
        check_vma=False,
    )
```

profile of v0, /device:TPU:0, one launch (start us, length us, event | category | flops | bytes accessed | tf_op | source)
XLA Modules:
  0.0 257.5 jit_solution(15649006521711701626)
XLA Ops:
  0.7 3.3 %slice.339 = bf16[6,16,64,1]{3,2,1,0:T(8,128)(2,1)} slice(bf16[6,16,64,256]{3,2,1,0:T(8,128)(2,1)} %param.7), slice={[0:6], [0:16], [0:64], [255:256]} | slice | bytes 24576 | tf_op jit(solution)/shard_map/slice | solution.py:73
  3.9 1.9 copy.21
  5.8 3.0 %collective-permute-start.1 = (bf16[6,16,64,1]{2,1,3,0:T(8,128)(2,1)S(1)}, bf16[6,16,64,1]{2,1,3,0:T(8,128)(2,1)S(1)}, u32[]{:S(2)}, u32[]{:S(2)}) collective-permute-start(bf16[6,16,64,1]{2,1,3,0:T(8,128)(2,1)S(1)} %copy.21), channel_id=1, source_target_pairs={{0,4},{4,8},{8,12},{12,16},{16,20},{20,24},{24,28},{28,0},{1,5},{5... | collective-permute-start | bytes 36872 | tf_op jit(solution)/shard_map/ppermute | solution.py:26
  8.8 1.2 fusion.92
  9.9 3.1 %collective-permute-start = (f32[16,64,1]{2,1,0:T(8,128)}, f32[16,64,1]{2,1,0:T(8,128)S(1)}, u32[]{:S(2)}, u32[]{:S(2)}) collective-permute-start(f32[16,64,1]{2,1,0:T(8,128)} %get-tuple-element.37), channel_id=1, source_target_pairs={{4,0},{8,4},{12,8},{16,12},{20,16},{24,20},{28,24},{0,28},{5,1},{9... | collective-permute-start | bytes 12296 | tf_op jit(solution)/shard_map/ppermute | solution.py:16
  13.0 1.1 slice.347
  14.1 1.5 collective-permute-start.4
  15.6 4.9 %convert_multiply_fusion.6 = (f32[16,64,256]{2,1,0:T(8,128)}, f32[16,64,256]{2,1,0:T(8,128)}, f32[16,64,256]{2,1,0:T(8,128)}, f32[16,64,256]{2,1,0:T(8,128)}, f32[16,64,256]{2,1,0:T(8,128)}, /*index=5*/f32[16,64,256]{2,1,0:T(8,128)}) fusion(bf16[6,16,64,256]{3,2,1,0:T(8,128)(2,1)} %param.8, f32[64]{0:T(128)S(1)} %not_convert_fusion), kind=kLoop, calls=%fused_computation.140 | loop fusion | flops 3145728 | bytes 9437440 | tf_op jit(solution)/shard_map/mul | solution.py:82
  20.5 2.8 %bitcast_convert_fusion = (f32[16,64,256]{2,1,0:T(8,128)}, f32[16,64,256]{2,1,0:T(8,128)}, f32[16,64,256]{2,1,0:T(8,128)}, f32[16,64,256]{2,1,0:T(8,128)}, f32[16,64,256]{2,1,0:T(8,128)}, /*index=5*/f32[16,64,256]{2,1,0:T(8,128)}) fusion(bf16[6,16,64,256]{3,2,1,0:T(8,128)(2,1)S(1)} %copy-done.1), kind=kLoop, calls=%fused_computation.158 | loop fusion | flops 1572864 | bytes 9437184 | tf_op jit(solution)/shard_map/convert_element_type | solution.py:80
  23.3 12.0 %collective-permute-done = f32[16,64,1]{2,1,0:T(8,128)S(1)} collective-permute-done((f32[16,64,1]{2,1,0:T(8,128)}, f32[16,64,1]{2,1,0:T(8,128)S(1)}, u32[]{:S(2)}, u32[]{:S(2)}) %collective-permute-start) | collective-permute-done | bytes 4128 | tf_op jit(solution)/shard_map/ppermute | solution.py:16
  35.3 1.2 pad_maximum_fusion.65
  36.5 0.6 collective-permute-start.3
  37.5 1.1 collective-permute-done.3
  38.6 1.7 collective-permute-done.5
  40.4 3.5 %fusion.62 = f32[16,64,256]{2,1,0:T(8,128)S(1)} fusion(f32[16,64,256]{2,1,0:T(8,128)S(1)} %copy-done.7, f32[16,1,258]{2,1,0:T(1,128)S(1)} %collective-permute-done.5, f32[16,64,1]{2,1,0:T(8,128)} %copy-done.8, f32[16,64,1]{2,1,0:T(8,128)} %collective-permute-done.2, f32[16,1,258]{2,1,0:T(1,128)S(1)} %collective-permute-done.3, f32[16,64,255]{2,1,0:T(8,128)} %bitcast.151, ...), kind=kLoop, calls=%fused_computation.111 | loop fusion | flops 7602176 | bytes 5284352 | tf_op jit(solution)/shard_map/add | solution.py:52
  44.5 4.0 %collective-permute-start.6 = (f32[16,64,1]{2,1,0:T(8,128)S(1)}, f32[16,64,1]{2,1,0:T(8,128)S(1)}, u32[]{:S(2)}, u32[]{:S(2)}) collective-permute-start(f32[16,64,1]{2,1,0:T(8,128)S(1)} %get-tuple-element.35), channel_id=1, source_target_pairs={{4,0},{8,4},{12,8},{16,12},{20,16},{24,20},{28,24},{0,28},{5,1},{9... | collective-permute-start | bytes 12296 | tf_op jit(solution)/shard_map/ppermute | solution.py:16
  48.5 20.7 %collective-permute-done.6 = f32[16,64,1]{2,1,0:T(8,128)S(1)} collective-permute-done((f32[16,64,1]{2,1,0:T(8,128)S(1)}, f32[16,64,1]{2,1,0:T(8,128)S(1)}, u32[]{:S(2)}, u32[]{:S(2)}) %collective-permute-start.6) | collective-permute-done | bytes 4128 | tf_op jit(solution)/shard_map/ppermute | solution.py:16
  69.6 1.4 collective-permute-start.8
  71.2 1.3 collective-permute-done.8
  72.6 1.6 collective-permute-done.9
  74.2 3.5 %fusion.50 = f32[16,64,256]{2,1,0:T(8,128)S(1)} fusion(f32[16,64,256]{2,1,0:T(8,128)S(1)} %pad_subtract_fusion.5, f32[16,1,258]{2,1,0:T(1,128)S(1)} %collective-permute-done.9, f32[16,64,1]{2,1,0:T(8,128)} %copy-done.11, f32[16,64,1]{2,1,0:T(8,128)} %copy-done.15, f32[16,1,258]{2,1,0:T(1,128)S(1)} %collective-permute-done.8, f32[16,64,255]{2,1,0:T(8,128)} %bitcast.149, ...), kind=kLoop, calls=%fused_computation.91 | loop fusion | flops 7602176 | bytes 5284352 | tf_op jit(solution)/shard_map/add | solution.py:52
  78.3 3.2 %collective-permute-start.10 = (f32[16,64,1]{2,1,0:T(8,128)S(1)}, f32[16,64,1]{2,1,0:T(8,128)S(1)}, u32[]{:S(2)}, u32[]{:S(2)}) collective-permute-start(f32[16,64,1]{2,1,0:T(8,128)S(1)} %get-tuple-element.33), channel_id=1, source_target_pairs={{4,0},{8,4},{12,8},{16,12},{20,16},{24,20},{28,24},{0,28},{5,1},{9... | collective-permute-start | bytes 12296 | tf_op jit(solution)/shard_map/ppermute | solution.py:16
  81.5 21.5 %collective-permute-done.10 = f32[16,64,1]{2,1,0:T(8,128)S(1)} collective-permute-done((f32[16,64,1]{2,1,0:T(8,128)S(1)}, f32[16,64,1]{2,1,0:T(8,128)S(1)}, u32[]{:S(2)}, u32[]{:S(2)}) %collective-permute-start.10) | collective-permute-done | bytes 4128 | tf_op jit(solution)/shard_map/ppermute | solution.py:16
  103.3 1.3 collective-permute-start.12
  104.8 1.3 collective-permute-done.12
  106.1 1.7 collective-permute-done.13
  107.8 5.7 %fusion.38 = f32[16,64,256]{2,1,0:T(8,128)S(1)} fusion(f32[16,64,256]{2,1,0:T(8,128)} %copy-done.3, f32[16,1,258]{2,1,0:T(1,128)S(1)} %collective-permute-done.13, f32[16,64,1]{2,1,0:T(8,128)} %copy-done.12, f32[16,64,1]{2,1,0:T(8,128)} %copy-done.16, f32[16,1,258]{2,1,0:T(1,128)S(1)} %collective-permute-done.12, f32[16,64,255]{2,1,0:T(8,128)} %bitcast.147, ...), kind=kLoop, calls=%fused_computation.71 | loop fusion | flops 7602176 | bytes 5284352 | tf_op jit(solution)/shard_map/add | solution.py:52
  114.2 2.2 collective-permute-start.14
  116.7 22.3 %collective-permute-done.14 = f32[16,64,1]{2,1,0:T(8,128)S(1)} collective-permute-done((f32[16,64,1]{2,1,0:T(8,128)S(1)}, f32[16,64,1]{2,1,0:T(8,128)S(1)}, u32[]{:S(2)}, u32[]{:S(2)}) %collective-permute-start.14) | collective-permute-done | bytes 4128 | tf_op jit(solution)/shard_map/ppermute | solution.py:16
  139.2 0.8 collective-permute-start.16
  140.3 1.2 collective-permute-done.16
  141.6 1.7 collective-permute-done.17
  143.3 5.6 %fusion.26 = f32[16,64,256]{2,1,0:T(8,128)S(1)} fusion(f32[16,64,256]{2,1,0:T(8,128)} %copy-done.4, f32[16,1,258]{2,1,0:T(1,128)S(1)} %collective-permute-done.17, f32[16,64,1]{2,1,0:T(8,128)} %copy-done.13, f32[16,64,1]{2,1,0:T(8,128)} %copy-done.17, f32[16,1,258]{2,1,0:T(1,128)S(1)} %collective-permute-done.16, f32[16,64,255]{2,1,0:T(8,128)} %bitcast.145, ...), kind=kLoop, calls=%fused_computation.51 | loop fusion | flops 7602176 | bytes 5284352 | tf_op jit(solution)/shard_map/add | solution.py:52
  149.5 2.1 collective-permute-start.18
  151.6 22.7 %collective-permute-done.18 = f32[16,64,1]{2,1,0:T(8,128)S(1)} collective-permute-done((f32[16,64,1]{2,1,0:T(8,128)S(1)}, f32[16,64,1]{2,1,0:T(8,128)S(1)}, u32[]{:S(2)}, u32[]{:S(2)}) %collective-permute-start.18) | collective-permute-done | bytes 4128 | tf_op jit(solution)/shard_map/ppermute | solution.py:16
  175.6 0.6 collective-permute-done.20
  176.2 2.0 collective-permute-done.21
  178.1 5.4 %fusion.14 = f32[16,64,256]{2,1,0:T(8,128)S(1)} fusion(f32[16,64,256]{2,1,0:T(8,128)} %copy-done.5, f32[16,1,258]{2,1,0:T(1,128)S(1)} %collective-permute-done.21, f32[16,64,1]{2,1,0:T(8,128)} %copy-done.14, f32[16,64,1]{2,1,0:T(8,128)} %copy-done.18, f32[16,1,258]{2,1,0:T(1,128)S(1)} %collective-permute-done.20, f32[16,64,255]{2,1,0:T(8,128)} %bitcast.143, ...), kind=kLoop, calls=%fused_computation.31 | loop fusion | flops 7602176 | bytes 5284352 | tf_op jit(solution)/shard_map/add | solution.py:52
  184.2 3.3 %collective-permute-start.22 = (f32[16,64,1]{2,1,0:T(8,128)S(1)}, f32[16,64,1]{2,1,0:T(8,128)S(1)}, u32[]{:S(2)}, u32[]{:S(2)}) collective-permute-start(f32[16,64,1]{2,1,0:T(8,128)S(1)} %get-tuple-element.27), channel_id=1, source_target_pairs={{4,0},{8,4},{12,8},{16,12},{20,16},{24,20},{28,24},{0,28},{5,1},{9... | collective-permute-start | bytes 12296 | tf_op jit(solution)/shard_map/ppermute | solution.py:16
  187.5 20.9 %collective-permute-done.22 = f32[16,64,1]{2,1,0:T(8,128)S(1)} collective-permute-done((f32[16,64,1]{2,1,0:T(8,128)S(1)}, f32[16,64,1]{2,1,0:T(8,128)S(1)}, u32[]{:S(2)}, u32[]{:S(2)}) %collective-permute-start.22) | collective-permute-done | bytes 4128 | tf_op jit(solution)/shard_map/ppermute | solution.py:16
  208.8 0.9 collective-permute-start.24
  209.9 1.3 collective-permute-done.24
  211.1 1.7 collective-permute-done.25
  212.9 5.4 %fusion.2 = f32[16,64,256]{2,1,0:T(8,128)S(1)} fusion(f32[16,64,256]{2,1,0:T(8,128)} %copy-done.6, f32[16,1,258]{2,1,0:T(1,128)S(1)} %collective-permute-done.25, f32[16,64,1]{2,1,0:T(8,128)} %copy-done.9, f32[16,64,1]{2,1,0:T(8,128)} %copy-done.10, f32[16,1,258]{2,1,0:T(1,128)S(1)} %collective-permute-done.24, f32[16,64,255]{2,1,0:T(8,128)} %bitcast.141, ...), kind=kLoop, calls=%fused_computation.11 | loop fusion | flops 7602176 | bytes 5284352 | tf_op jit(solution)/shard_map/add | solution.py:52
  218.6 1.3 fusion.74
  219.9 30.9 %all-gather = bf16[1,64,2048]{2,1,0:T(8,128)(2,1)S(1)} all-gather(bf16[1,64,256]{2,1,0:T(8,128)(2,1)S(1)} %fusion.74), channel_id=2, replica_groups=mesh['lon'=8,'lat'=4] {'lon'}, dimensions={2}, use_global_device_ids=true | all-gather | bytes 294912 | tf_op jit(solution)/shard_map/all_gather | solution.py:101
  251.3 5.4 %all_gather.7 = bf16[256,256]{1,0:T(8,128)(2,1)S(1)} all-gather(bf16[64,256]{1,0:T(8,128)(2,1)S(1)} %convolution_convert_fusion), channel_id=1, replica_groups=mesh['lon'=8,'lat'=4] {'lat'}, dimensions={0}, use_global_device_ids=true | all-gather | bytes 163840 | tf_op jit(solution)/shard_map/all_gather | solution.py:108
  256.7 0.8 convolution_bitcast_fusion
  (95 shorter events, 7.7 us)
Async XLA Ops:
  0.6 250.2 %copy-start = (bf16[256,2048]{1,0:T(8,128)(2,1)S(1)}, bf16[256,2048]{1,0:T(8,128)(2,1)}, u32[]{:S(2)}) copy-start(bf16[256,2048]{1,0:T(8,128)(2,1)} %param.10) | copy-start | bytes 3145732
  0.6 8.1 %copy-start.7 = (f32[16,64,256]{2,1,0:T(8,128)S(1)}, f32[16,64,256]{2,1,0:T(8,128)}, u32[]{:S(2)}) copy-start(f32[16,64,256]{2,1,0:T(8,128)} %param.6) | copy-start | bytes 3145732
  5.8 31.3 %collective-permute-start.1 = (bf16[6,16,64,1]{2,1,3,0:T(8,128)(2,1)S(1)}, bf16[6,16,64,1]{2,1,3,0:T(8,128)(2,1)S(1)}, u32[]{:S(2)}, u32[]{:S(2)}) collective-permute-start(bf16[6,16,64,1]{2,1,3,0:T(8,128)(2,1)S(1)} %copy.21), channel_id=1, source_target_pairs={{0,4},{4,8},{8,12},{12,16},{16,20},{20,24},{24,28},{28,0},{1,5},{5... | collective-permute-start | bytes 36872 | tf_op jit(solution)/shard_map/ppermute | solution.py:26
  9.9 25.4 %collective-permute-start = (f32[16,64,1]{2,1,0:T(8,128)}, f32[16,64,1]{2,1,0:T(8,128)S(1)}, u32[]{:S(2)}, u32[]{:S(2)}) collective-permute-start(f32[16,64,1]{2,1,0:T(8,128)} %get-tuple-element.37), channel_id=1, source_target_pairs={{4,0},{8,4},{12,8},{16,12},{20,16},{24,20},{28,24},{0,28},{5,1},{9... | collective-permute-start | bytes 12296 | tf_op jit(solution)/shard_map/ppermute | solution.py:16
  13.0 22.3 %collective-permute-start.2 = (f32[16,64,1]{2,1,0:T(8,128)}, f32[16,64,1]{2,1,0:T(8,128)}, u32[]{:S(2)}, u32[]{:S(2)}) collective-permute-start(f32[16,64,1]{2,1,0:T(8,128)} %get-tuple-element.36), channel_id=1, source_target_pairs={{0,4},{4,8},{8,12},{12,16},{16,20},{20,24},{24,28},{28,0},{1,5},{5... | collective-permute-start | bytes 12296 | tf_op jit(solution)/shard_map/ppermute | solution.py:14
  14.1 23.3 %collective-permute-start.4 = (bf16[6,16,1,256]{3,2,1,0:T(2,128)(2,1)S(1)}, bf16[6,16,1,256]{3,2,1,0:T(2,128)(2,1)S(1)}, u32[]{:S(2)}, u32[]{:S(2)}) collective-permute-start(bf16[6,16,1,256]{3,2,1,0:T(2,128)(2,1)S(1)} %slice.347), channel_id=1, source_target_pairs={{0,1},{1,2},{2,3},{4,5},{5,6},{6,7},{8,9},{9,10},{10,11},{12,13},{... | collective-permute-start | bytes 147464 | tf_op jit(solution)/shard_map/ppermute | solution.py:32
  15.6 4.9 %copy-start.1 = (bf16[6,16,64,256]{3,2,1,0:T(8,128)(2,1)S(1)}, bf16[6,16,64,256]{3,2,1,0:T(8,128)(2,1)}, u32[]{:S(2)}) copy-start(bf16[6,16,64,256]{3,2,1,0:T(8,128)(2,1)} %param.7) | copy-start | bytes 9437188
  35.3 1.8 copy-start.8
  36.5 2.1 collective-permute-start.3
  37.1 3.3 %collective-permute-start.5 = (f32[16,1,258]{2,1,0:T(1,128)S(1)}, f32[16,1,258]{2,1,0:T(1,128)S(1)}, u32[]{:S(2)}, u32[]{:S(2)}) collective-permute-start(f32[16,1,258]{2,1,0:T(1,128)S(1)} %get-tuple-element.25), channel_id=1, source_target_pairs={{0,1},{1,2},{2,3},{3,0},{4,5},{5,6},{6,7},{7,4},{8,9},{9,10},{10,1... | collective-permute-start | bytes 49544 | tf_op jit(solution)/shard_map/ppermute | solution.py:14
  40.4 3.5 %copy-start.2 = (bf16[15,64,256]{2,1,0:T(8,128)(2,1)S(1)}, bf16[15,64,256]{2,1,0:T(8,128)(2,1)}, u32[]{:S(2)}) copy-start(bf16[15,64,256]{2,1,0:T(8,128)(2,1)} %param.9) | copy-start | bytes 1474564
  44.5 24.7 %collective-permute-start.6 = (f32[16,64,1]{2,1,0:T(8,128)S(1)}, f32[16,64,1]{2,1,0:T(8,128)S(1)}, u32[]{:S(2)}, u32[]{:S(2)}) collective-permute-start(f32[16,64,1]{2,1,0:T(8,128)S(1)} %get-tuple-element.35), channel_id=1, source_target_pairs={{4,0},{8,4},{12,8},{16,12},{20,16},{24,20},{28,24},{0,28},{5,1},{9... | collective-permute-start | bytes 12296 | tf_op jit(solution)/shard_map/ppermute | solution.py:16
  48.5 20.8 %collective-permute-start.7 = (f32[16,64,1]{2,1,0:T(8,128)S(1)}, f32[16,64,1]{2,1,0:T(8,128)S(1)}, u32[]{:S(2)}, u32[]{:S(2)}) collective-permute-start(f32[16,64,1]{2,1,0:T(8,128)S(1)} %get-tuple-element.34), channel_id=1, source_target_pairs={{0,4},{4,8},{8,12},{12,16},{16,20},{20,24},{24,28},{28,0},{1,5},{5... | collective-permute-start | bytes 12296 | tf_op jit(solution)/shard_map/ppermute | solution.py:14
  69.2 1.8 copy-start.11
  69.4 1.6 copy-start.15
  69.6 3.0 %collective-permute-start.8 = (f32[16,1,258]{2,1,0:T(1,128)S(1)}, f32[16,1,258]{2,1,0:T(1,128)S(1)}, u32[]{:S(2)}, u32[]{:S(2)}) collective-permute-start(f32[16,1,258]{2,1,0:T(1,128)S(1)} %get-tuple-element.22), channel_id=1, source_target_pairs={{1,0},{2,1},{3,2},{0,3},{5,4},{6,5},{7,6},{4,7},{9,8},{10,9},{11,1... | collective-permute-start | bytes 49544 | tf_op jit(solution)/shard_map/ppermute | solution.py:16
  71.0 3.3 %collective-permute-start.9 = (f32[16,1,258]{2,1,0:T(1,128)S(1)}, f32[16,1,258]{2,1,0:T(1,128)S(1)}, u32[]{:S(2)}, u32[]{:S(2)}) collective-permute-start(f32[16,1,258]{2,1,0:T(1,128)S(1)} %get-tuple-element.23), channel_id=1, source_target_pairs={{0,1},{1,2},{2,3},{3,0},{4,5},{5,6},{6,7},{7,4},{8,9},{9,10},{10,1... | collective-permute-start | bytes 49544 | tf_op jit(solution)/shard_map/ppermute | solution.py:14
  78.1 25.0 %copy-start.3 = (f32[16,64,256]{2,1,0:T(8,128)}, f32[16,64,256]{2,1,0:T(8,128)S(1)}, u32[]{:S(2)}) copy-start(f32[16,64,256]{2,1,0:T(8,128)S(1)} %pad_subtract_fusion.4) | copy-start | bytes 3145732
  78.3 24.7 %collective-permute-start.10 = (f32[16,64,1]{2,1,0:T(8,128)S(1)}, f32[16,64,1]{2,1,0:T(8,128)S(1)}, u32[]{:S(2)}, u32[]{:S(2)}) collective-permute-start(f32[16,64,1]{2,1,0:T(8,128)S(1)} %get-tuple-element.33), channel_id=1, source_target_pairs={{4,0},{8,4},{12,8},{16,12},{20,16},{24,20},{28,24},{0,28},{5,1},{9... | collective-permute-start | bytes 12296 | tf_op jit(solution)/shard_map/ppermute | solution.py:16
  81.5 21.5 %collective-permute-start.11 = (f32[16,64,1]{2,1,0:T(8,128)S(1)}, f32[16,64,1]{2,1,0:T(8,128)S(1)}, u32[]{:S(2)}, u32[]{:S(2)}) collective-permute-start(f32[16,64,1]{2,1,0:T(8,128)S(1)} %get-tuple-element.32), channel_id=1, source_target_pairs={{0,4},{4,8},{8,12},{12,16},{16,20},{20,24},{24,28},{28,0},{1,5},{5... | collective-permute-start | bytes 12296 | tf_op jit(solution)/shard_map/ppermute | solution.py:14
  103.0 1.5 copy-start.12
  103.0 1.5 copy-start.16
  103.3 2.8 %collective-permute-start.12 = (f32[16,1,258]{2,1,0:T(1,128)S(1)}, f32[16,1,258]{2,1,0:T(1,128)S(1)}, u32[]{:S(2)}, u32[]{:S(2)}) collective-permute-start(f32[16,1,258]{2,1,0:T(1,128)S(1)} %get-tuple-element.20), channel_id=1, source_target_pairs={{1,0},{2,1},{3,2},{0,3},{5,4},{6,5},{7,6},{4,7},{9,8},{10,9},{11,1... | collective-permute-start | bytes 49544 | tf_op jit(solution)/shard_map/ppermute | solution.py:16
  104.6 3.3 %collective-permute-start.13 = (f32[16,1,258]{2,1,0:T(1,128)S(1)}, f32[16,1,258]{2,1,0:T(1,128)S(1)}, u32[]{:S(2)}, u32[]{:S(2)}) collective-permute-start(f32[16,1,258]{2,1,0:T(1,128)S(1)} %get-tuple-element.21), channel_id=1, source_target_pairs={{0,1},{1,2},{2,3},{3,0},{4,5},{5,6},{6,7},{7,4},{8,9},{9,10},{10,1... | collective-permute-start | bytes 49544 | tf_op jit(solution)/shard_map/ppermute | solution.py:14
  114.0 25.1 %copy-start.4 = (f32[16,64,256]{2,1,0:T(8,128)}, f32[16,64,256]{2,1,0:T(8,128)S(1)}, u32[]{:S(2)}) copy-start(f32[16,64,256]{2,1,0:T(8,128)S(1)} %pad_subtract_fusion.3) | copy-start | bytes 3145732
  114.2 24.8 %collective-permute-start.14 = (f32[16,64,1]{2,1,0:T(8,128)S(1)}, f32[16,64,1]{2,1,0:T(8,128)S(1)}, u32[]{:S(2)}, u32[]{:S(2)}) collective-permute-start(f32[16,64,1]{2,1,0:T(8,128)S(1)} %get-tuple-element.31), channel_id=1, source_target_pairs={{4,0},{8,4},{12,8},{16,12},{20,16},{24,20},{28,24},{0,28},{5,1},{9... | collective-permute-start | bytes 12296 | tf_op jit(solution)/shard_map/ppermute | solution.py:16
  116.4 22.7 %collective-permute-start.15 = (f32[16,64,1]{2,1,0:T(8,128)S(1)}, f32[16,64,1]{2,1,0:T(8,128)S(1)}, u32[]{:S(2)}, u32[]{:S(2)}) collective-permute-start(f32[16,64,1]{2,1,0:T(8,128)S(1)} %get-tuple-element.30), channel_id=1, source_target_pairs={{0,4},{4,8},{8,12},{12,16},{16,20},{20,24},{24,28},{28,0},{1,5},{5... | collective-permute-start | bytes 12296 | tf_op jit(solution)/shard_map/ppermute | solution.py:14
  139.0 1.0 copy-start.13
  139.0 1.1 copy-start.17
  139.2 2.3 collective-permute-start.16
  140.0 3.3 %collective-permute-start.17 = (f32[16,1,258]{2,1,0:T(1,128)S(1)}, f32[16,1,258]{2,1,0:T(1,128)S(1)}, u32[]{:S(2)}, u32[]{:S(2)}) collective-permute-start(f32[16,1,258]{2,1,0:T(1,128)S(1)} %get-tuple-element.19), channel_id=1, source_target_pairs={{0,1},{1,2},{2,3},{3,0},{4,5},{5,6},{6,7},{7,4},{8,9},{9,10},{10,1... | collective-permute-start | bytes 49544 | tf_op jit(solution)/shard_map/ppermute | solution.py:14
  149.3 25.1 %copy-start.5 = (f32[16,64,256]{2,1,0:T(8,128)}, f32[16,64,256]{2,1,0:T(8,128)S(1)}, u32[]{:S(2)}) copy-start(f32[16,64,256]{2,1,0:T(8,128)S(1)} %pad_subtract_fusion.2) | copy-start | bytes 3145732
  149.5 24.9 %collective-permute-start.18 = (f32[16,64,1]{2,1,0:T(8,128)S(1)}, f32[16,64,1]{2,1,0:T(8,128)S(1)}, u32[]{:S(2)}, u32[]{:S(2)}) collective-permute-start(f32[16,64,1]{2,1,0:T(8,128)S(1)} %get-tuple-element.29), channel_id=1, source_target_pairs={{4,0},{8,4},{12,8},{16,12},{20,16},{24,20},{28,24},{0,28},{5,1},{9... | collective-permute-start | bytes 12296 | tf_op jit(solution)/shard_map/ppermute | solution.py:16
  151.6 22.7 %collective-permute-start.19 = (f32[16,64,1]{2,1,0:T(8,128)S(1)}, f32[16,64,1]{2,1,0:T(8,128)S(1)}, u32[]{:S(2)}, u32[]{:S(2)}) collective-permute-start(f32[16,64,1]{2,1,0:T(8,128)S(1)} %get-tuple-element.28), channel_id=1, source_target_pairs={{0,4},{4,8},{8,12},{12,16},{16,20},{20,24},{24,28},{28,0},{1,5},{5... | collective-permute-start | bytes 12296 | tf_op jit(solution)/shard_map/ppermute | solution.py:14
  174.4 0.8 copy-start.14
  174.4 1.0 copy-start.18
  174.6 1.6 collective-permute-start.20
  174.7 3.5 %collective-permute-start.21 = (f32[16,1,258]{2,1,0:T(1,128)S(1)}, f32[16,1,258]{2,1,0:T(1,128)S(1)}, u32[]{:S(2)}, u32[]{:S(2)}) collective-permute-start(f32[16,1,258]{2,1,0:T(1,128)S(1)} %get-tuple-element.17), channel_id=1, source_target_pairs={{0,1},{1,2},{2,3},{3,0},{4,5},{5,6},{6,7},{7,4},{8,9},{9,10},{10,1... | collective-permute-start | bytes 49544 | tf_op jit(solution)/shard_map/ppermute | solution.py:14
  184.0 24.6 %copy-start.6 = (f32[16,64,256]{2,1,0:T(8,128)}, f32[16,64,256]{2,1,0:T(8,128)S(1)}, u32[]{:S(2)}) copy-start(f32[16,64,256]{2,1,0:T(8,128)S(1)} %pad_subtract_fusion.1) | copy-start | bytes 3145732
  184.2 24.2 %collective-permute-start.22 = (f32[16,64,1]{2,1,0:T(8,128)S(1)}, f32[16,64,1]{2,1,0:T(8,128)S(1)}, u32[]{:S(2)}, u32[]{:S(2)}) collective-permute-start(f32[16,64,1]{2,1,0:T(8,128)S(1)} %get-tuple-element.27), channel_id=1, source_target_pairs={{4,0},{8,4},{12,8},{16,12},{20,16},{24,20},{28,24},{0,28},{5,1},{9... | collective-permute-start | bytes 12296 | tf_op jit(solution)/shard_map/ppermute | solution.py:16
  187.5 21.1 %collective-permute-start.23 = (f32[16,64,1]{2,1,0:T(8,128)S(1)}, f32[16,64,1]{2,1,0:T(8,128)S(1)}, u32[]{:S(2)}, u32[]{:S(2)}) collective-permute-start(f32[16,64,1]{2,1,0:T(8,128)S(1)} %get-tuple-element.26), channel_id=1, source_target_pairs={{0,4},{4,8},{8,12},{12,16},{16,20},{20,24},{24,28},{28,0},{1,5},{5... | collective-permute-start | bytes 12296 | tf_op jit(solution)/shard_map/ppermute | solution.py:14
  208.4 1.2 copy-start.9
  208.5 1.1 copy-start.10
  208.8 2.4 collective-permute-start.24
  209.6 3.3 %collective-permute-start.25 = (f32[16,1,258]{2,1,0:T(1,128)S(1)}, f32[16,1,258]{2,1,0:T(1,128)S(1)}, u32[]{:S(2)}, u32[]{:S(2)}) collective-permute-start(f32[16,1,258]{2,1,0:T(1,128)S(1)} %get-tuple-element.15), channel_id=1, source_target_pairs={{0,1},{1,2},{2,3},{3,0},{4,5},{5,6},{6,7},{7,4},{8,9},{9,10},{10,1... | collective-permute-start | bytes 49544 | tf_op jit(solution)/shard_map/ppermute | solution.py:14
  218.4 38.3 %copy-start.20 = (bf16[64,256]{1,0:T(8,128)(2,1)S(1)}, bf16[64,256]{1,0:T(8,128)(2,1)}, u32[]{:S(2)}) copy-start(bf16[64,256]{1,0:T(8,128)(2,1)} %param.11) | copy-start | bytes 98308
  218.6 38.8 %copy-start.19 = (f32[16,64,256]{2,1,0:T(8,128)}, f32[16,64,256]{2,1,0:T(8,128)S(1)}, u32[]{:S(2)}) copy-start(f32[16,64,256]{2,1,0:T(8,128)S(1)} %pad_subtract_fusion) | copy-start | bytes 3145732
where the time goes:
time: 258 us; the launch traced here: 257 us
  waiting for transfers between devices  138 us (53%)
  other arithmetic  42.6 us (17%)
  blocking collectives  36.3 us (14%)
  starting transfers between devices  28.2 us (11%)
  local copies, waits for them, and re-layouts  10.2 us (4%)
    ppermute x12, waiting for transfers between devices, with_halo(): lax.ppermute(head, axis, [((i + 1) % count, i) for i in range(count)])  127 us
    all_gather x1, blocking collectives, per_device(): lax.all_gather(surface, 'lon', axis=1, tiled=True)  30.9 us
    add x6, other arithmetic, transport(): adjoint + jnp.maximum(east_face, 0.0) * (east_side - adjoint)  29.2 us
    ppermute x12, starting transfers between devices, with_halo(): lax.ppermute(head, axis, [((i + 1) % count, i) for i in range(count)])  22.9 us
    ppermute x12, waiting for transfers between devices, with_halo(): lax.ppermute(tail, axis, [(i, (i + 1) % count) for i in range(count)])  10.9 us
    all_gather x1, blocking collectives, per_device(): lax.all_gather(zonal, 'lat', axis=0, tiled=True)  5.43 us
  transfers between devices with their start and end apart: 26, of which 20 were waited for; matrix products, arithmetic and copies ran while one was open for 5% of the time, Pallas kernels for 0%

commit v1 on v0

v1 whole, which is shorter than its diff:
```python
import functools

import jax
import jax.numpy as jnp
from jax import lax
from jax.experimental import pallas as pl
from jax.experimental.pallas import tpu as pltpu
from jax.sharding import PartitionSpec as P

F32 = jnp.float32
BF16 = jnp.bfloat16
CHUNK = 16
LANES = 128
SUB = 8
TO_WEST, TO_EAST, TO_SOUTH, TO_NORTH, WIND_EAST, WIND_NORTH = 0, 2, 4, 5, 6, 8
KINDS = 9


def kernel(
    n_lon,
    n_lat,
    misfit,
    east,
    north,
    mixing,
    lon_corr,
    lat_corr,
    flux_out,
    state_out,
    state,
    grad,
    send_w,
    send_e,
    send_s,
    send_n,
    wind_e,
    wind_n,
    recv_e,
    recv_w,
    recv_n,
    recv_s,
    wind_w,
    wind_s,
    band,
    zonal,
    halo_send,
    halo_recv,
    lon_send,
    lon_recv,
    lat_send,
    lat_recv,
):
    steps = east.shape[0]
    levels, rows, cols = misfit.shape
    chunks = rows // CHUNK
    per = chunks // 2 * (CHUNK // SUB)
    order = (0, chunks - 1) + tuple(range(1, chunks - 1))
    groups = (order[: chunks // 2], order[chunks // 2 :])
    lon = lax.axis_index("lon")
    lat = lax.axis_index("lat")
    west = {"lon": lax.rem(lon + n_lon - 1, n_lon)}
    east_id = {"lon": lax.rem(lon + 1, n_lon)}
    south = {"lat": lax.rem(lat + n_lat - 1, n_lat)}
    north_id = {"lat": lax.rem(lat + 1, n_lat)}
    lane = lax.broadcasted_iota(jnp.int32, (SUB, LANES), 1)
    lane2 = lax.broadcasted_iota(jnp.int32, (CHUNK, LANES), 1)
    row2 = lax.broadcasted_iota(jnp.int32, (CHUNK, cols), 0)
    top = lat == n_lat - 1
    keep_south = jnp.where(lat == 0, 0.0, 1.0).astype(F32)

    def copy(src, dst, k, kind, target):
        return pltpu.make_async_remote_copy(
            src_ref=src,
            dst_ref=dst,
            send_sem=halo_send.at[k, kind],
            recv_sem=halo_recv.at[k, kind],
            device_id=target,
            device_id_type=pl.DeviceIdType.MESH,
        )

    def to_west(k, g):
        return copy(send_w.at[k, g], recv_e.at[k, g], k, TO_WEST + g, west)

    def to_east(k, g):
        return copy(send_e.at[k, g], recv_w.at[k, g], k, TO_EAST + g, east_id)

    def to_south(k):
        return copy(send_s.at[k], recv_n.at[k], k, TO_SOUTH, south)

    def to_north(k):
        return copy(send_n.at[k], recv_s.at[k], k, TO_NORTH, north_id)

    def wind_east(k, g):
        return copy(wind_e.at[k, g], wind_w.at[k, g], k, WIND_EAST + g, east_id)

    def wind_north(k):
        return copy(wind_n.at[k], wind_s.at[k], k, WIND_NORTH, north_id)

    def packed(pack, column, level, place):
        for j in range(CHUNK // SUB):
            tile = jnp.broadcast_to(column[j * SUB : (j + 1) * SUB], (SUB, LANES))
            pack = jnp.where(lane == level * per + place * (CHUNK // SUB) + j, tile, pack)
        return pack

    def unpacked(pack, level, place):
        base = level * per + place * (CHUNK // SUB)
        return jnp.concatenate(
            [
                jnp.broadcast_to(pack[:, base + j : base + j + 1], (SUB, LANES))
                for j in range(CHUNK // SUB)
            ],
            axis=0,
        )

    def pack_winds(k):
        n = steps - 1 - k
        for g, members in enumerate(groups):
            pack = jnp.zeros((SUB, LANES), F32)
            for place, c in enumerate(members):
                for level in range(levels):
                    tile = east[n, level, c * CHUNK : (c + 1) * CHUNK, cols - LANES :]
                    pack = packed(pack, tile.astype(F32)[:, LANES - 1 :], level, place)
            wind_e[k, g] = pack
        edge = [
            north[n, level, rows - CHUNK :, :].astype(F32)[CHUNK - 1 :] for level in range(levels)
        ]
        wind_n[k] = jnp.concatenate(edge, axis=0).astype(BF16)

    def send_winds(k):
        wind_east(k, 0).start()
        wind_east(k, 1).start()
        wind_north(k).start()

    state[0] = misfit[...]
    for g, members in enumerate(groups):
        pack_w = jnp.zeros((SUB, LANES), F32)
        pack_e = jnp.zeros((SUB, LANES), F32)
        for place, c in enumerate(members):
            for level in range(levels):
                part = slice(c * CHUNK, (c + 1) * CHUNK)
                pack_w = packed(pack_w, misfit[level, part, :LANES][:, :1], level, place)
                pack_e = packed(
                    pack_e, misfit[level, part, cols - LANES :][:, LANES - 1 :], level, place
                )
        send_w[0, g] = pack_w
        send_e[0, g] = pack_e
    for level in range(levels):
        send_s[0, level : level + 1, :] = misfit[level, 0:1, :]
        send_n[0, level : level + 1, :] = misfit[level, rows - 1 : rows, :]
    pack_winds(0)
    grad[...] = jnp.zeros_like(grad)

    barrier = pltpu.get_barrier_semaphore()
    for d in range(1, n_lon):
        pl.semaphore_signal(
            barrier,
            inc=1,
            device_id={"lon": lax.rem(lon + d, n_lon)},
            device_id_type=pl.DeviceIdType.MESH,
        )
    for d in range(1, n_lat):
        pl.semaphore_signal(
            barrier,
            inc=1,
            device_id={"lat": lax.rem(lat + d, n_lat)},
            device_id_type=pl.DeviceIdType.MESH,
        )
    pl.semaphore_wait(barrier, n_lon + n_lat - 2)

    for g in range(2):
        to_west(0, g).start()
        to_east(0, g).start()
        if g == 0:
            to_south(0).start()
            to_north(0).start()
            send_winds(0)

    def work(k, g):
        n = steps - 1 - k
        cur = lax.rem(k, 2)
        new = 1 - cur
        halo_e = recv_e[k, g]
        west_term = jnp.minimum(wind_w[k, g], 0.0) * (send_w[k, g] - recv_w[k, g])
        pack_w = jnp.zeros((SUB, LANES), F32)
        pack_e = jnp.zeros((SUB, LANES), F32)
        if g == 0:
            wind_row = wind_s[k].astype(F32) * keep_south
        for place, c in enumerate(groups[g]):
            r = c * CHUNK
            part = slice(r, r + CHUNK)

            def finish(level, value, pack_w, pack_e):
                state[new, level, part, :] = value
                if level == 0:
                    grad[part, :] += value
                pack_w = packed(pack_w, value[:, :1], level, place)
                pack_e = packed(pack_e, value[:, cols - 1 :], level, place)
                later = jnp.minimum(k + 1, steps)
                if c == 0:
                    send_s[later, level : level + 1, :] = value[0:1, :]
                if c == chunks - 1:
                    send_n[later, level : level + 1, :] = value[CHUNK - 1 :, :]
                return pack_w, pack_e

            before = flux = None
            for level in range(levels):
                adj = state[cur, level, part, :]
                ue = east[n, level, part, :].astype(F32)
                vn = north[n, level, part, :].astype(F32)
                ahead = pltpu.roll(adj, cols - 1, 1)
                right = jnp.where(
                    lane2 == LANES - 1, unpacked(halo_e, level, place), ahead[:, cols - LANES :]
                )
                d = jnp.concatenate([ahead[:, : cols - LANES], right], axis=1) - adj
                back = pltpu.roll(jnp.minimum(ue, 0.0) * d, 1, 1)
                left = jnp.where(lane2 == 0, unpacked(west_term, level, place), back[:, :LANES])
                back = jnp.concatenate([left, back[:, LANES:]], axis=1)
                a = adj + jnp.maximum(ue, 0.0) * d + back
                if c == chunks - 1:
                    vn = jnp.where(jnp.logical_and(row2 == CHUNK - 1, top), 0.0, vn)
                    above = recv_n[k, level : level + 1, :]
                else:
                    above = state[cur, level, r + CHUNK : r + CHUNK + 1, :]
                d = jnp.where(row2 == CHUNK - 1, above, pltpu.roll(adj, CHUNK - 1, 0)) - adj
                if c == 0:
                    below = recv_s[k, level : level + 1, :]
                    vs = wind_row[level : level + 1, :]
                else:
                    below = state[cur, level, r - 1 : r, :]
                    vs = north[n, level, r - CHUNK : r, :].astype(F32)[CHUNK - 1 :]
                edge = jnp.minimum(vs, 0.0) * (adj[0:1] - below)
                a = a + jnp.maximum(vn, 0.0) * d
                a = a + jnp.where(row2 == 0, edge, pltpu.roll(jnp.minimum(vn, 0.0) * d, 1, 0))
                if level > 0:
                    flow = mixing[level - 1, part, :].astype(F32) * (a - before)
                    value = before + flow
                    if flux is not None:
                        value = value - flux
                    pack_w, pack_e = finish(level - 1, value, pack_w, pack_e)
                    flux = flow
                before = a
            pack_w, pack_e = finish(levels - 1, before - flux, pack_w, pack_e)
        later = jnp.minimum(k + 1, steps)
        send_w[later, g] = pack_w
        send_e[later, g] = pack_e

    def step(k, carry):
        @pl.when(k + 1 < steps)
        def _():
            pack_winds(k + 1)
            send_winds(k + 1)

        to_west(k, 0).wait_recv()
        to_east(k, 0).wait_recv()
        to_south(k).wait_recv()
        to_north(k).wait_recv()
        wind_east(k, 0).wait_recv()
        wind_north(k).wait_recv()
        work(k, 0)

        @pl.when(k + 1 < steps)
        def _():
            to_south(k + 1).start()
            to_north(k + 1).start()
            to_west(k + 1, 0).start()
            to_east(k + 1, 0).start()

        to_west(k, 1).wait_recv()
        to_east(k, 1).wait_recv()
        wind_east(k, 1).wait_recv()
        work(k, 1)

        @pl.when(k + 1 < steps)
        def _():
            to_west(k + 1, 1).start()
            to_east(k + 1, 1).start()

        return carry

    lax.fori_loop(0, steps, step, 0)

    band[lon] = (grad[...] / steps).astype(BF16)

    def spread(d):
        return pltpu.make_async_remote_copy(
            src_ref=band.at[lon],
            dst_ref=band.at[lon],
            send_sem=lon_send.at[d],
            recv_sem=lon_recv.at[d],
            device_id={"lon": lax.rem(lon + d, n_lon)},
            device_id_type=pl.DeviceIdType.MESH,
        )

    for d in range(1, n_lon):
        spread(d).start()

    def product(d):
        src = lax.rem(lon + n_lon - d, n_lon)
        block = lon_corr[:, pl.ds(pl.multiple_of(src * cols, cols), cols)]
        return lax.dot_general(
            band[src], block, (((1,), (1,)), ((), ())), preferred_element_type=F32
        )

    total = product(0)
    state_out[...] = state[steps % 2]
    for d in range(1, n_lon):
        spread(d).wait_recv()
        total = total + product(d)

    mine = pl.ds(pl.multiple_of(lat * rows, rows), rows)
    zonal[mine, :] = total.astype(BF16)

    def share(d):
        return pltpu.make_async_remote_copy(
            src_ref=zonal.at[mine],
            dst_ref=zonal.at[mine],
            send_sem=lat_send.at[d],
            recv_sem=lat_recv.at[d],
            device_id={"lat": lax.rem(lat + d, n_lat)},
            device_id_type=pl.DeviceIdType.MESH,
        )

    for d in range(1, n_lat):
        share(d).start()

    def settle(k, carry):
        for g in range(2):
            to_west(k, g).wait_send()
            to_east(k, g).wait_send()
            wind_east(k, g).wait_send()
        to_south(k).wait_send()
        to_north(k).wait_send()
        wind_north(k).wait_send()
        return carry

    lax.fori_loop(0, steps, settle, 0)
    for d in range(1, n_lon):
        spread(d).wait_send()
    for d in range(1, n_lat):
        share(d).wait_recv()
    flux_out[...] = jnp.dot(lat_corr[...], zonal[...], preferred_element_type=F32)
    for d in range(1, n_lat):
        share(d).wait_send()


def per_device(n_lon, n_lat, misfit, east_wind, north_wind, mixing, lon_corr, lat_corr):
    steps = east_wind.shape[0]
    levels, rows, cols = misfit.shape
    pack = (steps, 2, SUB, LANES)
    pack_out = (steps + 1, 2, SUB, LANES)
    edge = (steps, levels, cols)
    edge_out = (steps + 1, levels, cols)
    vmem = pl.BlockSpec(memory_space=pltpu.VMEM)
    dma = pltpu.SemaphoreType.DMA
    return pl.pallas_call(
        functools.partial(kernel, n_lon, n_lat),
        out_shape=(
            jax.ShapeDtypeStruct((rows, cols), F32),
            jax.ShapeDtypeStruct(misfit.shape, F32),
        ),
        in_specs=[vmem] * 6,
        out_specs=(vmem, vmem),
        scratch_shapes=[
            pltpu.VMEM((2, levels, rows, cols), F32),
            pltpu.VMEM((rows, cols), F32),
            pltpu.VMEM(pack_out, F32),
            pltpu.VMEM(pack_out, F32),
            pltpu.VMEM(edge_out, F32),
            pltpu.VMEM(edge_out, F32),
            pltpu.VMEM(pack, F32),
            pltpu.VMEM(edge, BF16),
            pltpu.VMEM(pack, F32),
            pltpu.VMEM(pack, F32),
            pltpu.VMEM(edge, F32),
            pltpu.VMEM(edge, F32),
            pltpu.VMEM(pack, F32),
            pltpu.VMEM(edge, BF16),
            pltpu.VMEM((n_lon, rows, cols), BF16),
            pltpu.VMEM((n_lat * rows, cols), BF16),
            dma((steps, KINDS)),
            dma((steps, KINDS)),
            dma((n_lon,)),
            dma((n_lon,)),
            dma((n_lat,)),
            dma((n_lat,)),
        ],
        compiler_params=pltpu.CompilerParams(
            collective_id=0, has_side_effects=True, vmem_limit_bytes=40 * 1024 * 1024
        ),
    )(misfit, east_wind, north_wind, mixing, lon_corr, lat_corr)


def solution(mesh):
    placed = (
        P(None, "lat", "lon"),
        P(None, None, "lat", "lon"),
        P(None, None, "lat", "lon"),
        P(None, "lat", "lon"),
        P("lon", None),
        P("lat", None),
    )
    return jax.shard_map(
        functools.partial(per_device, mesh.shape["lon"], mesh.shape["lat"]),
        mesh=mesh,
        in_specs=placed,
        out_specs=(P("lat", "lon"), P(None, "lat", "lon")),
        check_vma=False,
    )
```

time: 258 us -> 77 us (0.30)
  waiting for transfers between devices: 138 us -> 0 us
  Pallas kernels: 0 us -> 66.3 us
  other arithmetic: 42.6 us -> 0 us
  blocking collectives: 36.3 us -> 0 us
  starting transfers between devices: 28.2 us -> 0 us
    ppermute x26 -> x0, waiting for transfers between devices: 138 us -> none  [the longest x12 127 us: with_halo(): lax.ppermute(head, axis, [((i + 1) % count, i) for i in range(count)])]
    pallas_call x0 -> x1, Pallas kernels: none -> 66.3 us  [per_device(): pl.pallas_call(functools.partial(kernel, n_lon, n_lat), out_shape=(jax.Sh...]
    all_gather x2 -> x0, blocking collectives: 36.3 us -> none  [the longest x1 30.9 us: per_device(): lax.all_gather(surface, 'lon', axis=1, tiled=True)]
    add x6 -> x0, other arithmetic: 29.2 us -> none  [transport(): adjoint + jnp.maximum(east_face, 0.0) * (east_side - adjoint)]
    ppermute x26 -> x0, starting transfers between devices: 28.2 us -> none  [the longest x12 22.9 us: with_halo(): lax.ppermute(head, axis, [((i + 1) % count, i) for i in range(count)])]
    unnamed x43 -> x14, local copies, waits for them, and re-layouts: 2.2 us -> 9.61 us
    slice x8 -> x0, local copies, waits for them, and re-layouts: 6.56 us -> none  [the longest x1 3.27 us: per_device(): west_all = shifted(east_wind[:, :, :, -1:], 'lon', 1)]
    mul x7 -> x0, other arithmetic: 5.76 us -> none  [the longest x1 4.87 us: per_device(): north_face = north_raw.astype(jnp.float32) * keep_north]
  transfers between devices with their start and end apart: 26 -> 0, of which waited for: 20 -> 0; matrix products, arithmetic and copies ran while one was open for 5% -> 0% of each run, Pallas kernels for 0% -> 0%
where the time goes in v1:
time: 77 us; the launch traced here: 76.6 us
  Pallas kernels  66.3 us (86%)
  local copies, waits for them, and re-layouts  9.61 us (12%)
    pallas_call x1, Pallas kernels, per_device(): pl.pallas_call(functools.partial(kernel, n_lon, n_lat), out_shape=(jax.Sh...  66.3 us
    unnamed x14, local copies, waits for them, and re-layouts  9.61 us

profile of v1, /device:TPU:0, one launch (start us, length us, event | category | flops | bytes accessed | tf_op | source)
XLA Modules:
  0.0 76.6 jit_solution(12296234839184186562)
XLA Ops:
  0.6 0.0 copy-start
  0.6 1.9 %copy-done = bf16[6,16,64,256]{3,2,1,0:T(8,128)(2,1)S(1)} copy-done((bf16[6,16,64,256]{3,2,1,0:T(8,128)(2,1)S(1)}, bf16[6,16,64,256]{3,2,1,0:T(8,128)(2,1)}, u32[]{:S(2)}) %copy-start) | copy-done | bytes 3145752
  2.5 0.0 copy-start.1
  2.5 1.9 %copy-done.1 = bf16[6,16,64,256]{3,2,1,0:T(8,128)(2,1)S(1)} copy-done((bf16[6,16,64,256]{3,2,1,0:T(8,128)(2,1)S(1)}, bf16[6,16,64,256]{3,2,1,0:T(8,128)(2,1)}, u32[]{:S(2)}) %copy-start.1) | copy-done | bytes 3145752
  4.4 0.0 copy-start.2
  4.4 1.2 %copy-done.2 = f32[16,64,256]{2,1,0:T(8,128)S(1)} copy-done((f32[16,64,256]{2,1,0:T(8,128)S(1)}, f32[16,64,256]{2,1,0:T(8,128)}, u32[]{:S(2)}) %copy-start.2) | copy-done | bytes 1048600
  5.6 0.0 copy-start.3
  5.6 1.2 %copy-done.3 = bf16[256,2048]{1,0:T(8,128)(2,1)S(1)} copy-done((bf16[256,2048]{1,0:T(8,128)(2,1)S(1)}, bf16[256,2048]{1,0:T(8,128)(2,1)}, u32[]{:S(2)}) %copy-start.3) | copy-done | bytes 1048600
  6.9 0.0 copy-start.4
  6.9 1.0 %copy-done.4 = bf16[15,64,256]{2,1,0:T(8,128)(2,1)S(1)} copy-done((bf16[15,64,256]{2,1,0:T(8,128)(2,1)S(1)}, bf16[15,64,256]{2,1,0:T(8,128)(2,1)}, u32[]{:S(2)}) %copy-start.4) | copy-done | bytes 491544
  7.9 0.0 copy-start.5
  7.9 0.8 copy-done.5
  8.7 66.3 %shard_map.77 = (f32[64,256]{1,0:T(8,128)S(1)}, f32[16,64,256]{2,1,0:T(8,128)S(1)}) custom-call(f32[16,64,256]{2,1,0:T(8,128)S(1)} %copy-done.2, bf16[6,16,64,256]{3,2,1,0:T(8,128)(2,1)S(1)} %copy-done, bf16[6,16,64,256]{3,2,1,0:T(8,128)(2,1)S(1)} %copy-done.1, bf16[15,64,256]{2,1,0:T(8,128)(2,1)S(1)} %copy-done.4, bf16[256,2048]{1,0:T(8,128)(2,1)S(1)} %copy-done.3, ...), custom_call_target="tpu_custom_call" | custom-call | tf_op jit(solution)/shard_map/pallas_call | solution.py:355
  75.0 0.6 copy.10
  75.6 1.0 %copy.11 = f32[16,64,256]{2,1,0:T(8,128)} copy(f32[16,64,256]{2,1,0:T(8,128)S(1)} %get-tuple-element.5) | data formatting | bytes 2097152
Async XLA Ops:
  0.6 1.9 %copy-start = (bf16[6,16,64,256]{3,2,1,0:T(8,128)(2,1)S(1)}, bf16[6,16,64,256]{3,2,1,0:T(8,128)(2,1)}, u32[]{:S(2)}) copy-start(bf16[6,16,64,256]{3,2,1,0:T(8,128)(2,1)} %east.1) | copy-start | bytes 9437188
  2.5 1.9 %copy-start.1 = (bf16[6,16,64,256]{3,2,1,0:T(8,128)(2,1)S(1)}, bf16[6,16,64,256]{3,2,1,0:T(8,128)(2,1)}, u32[]{:S(2)}) copy-start(bf16[6,16,64,256]{3,2,1,0:T(8,128)(2,1)} %north.1) | copy-start | bytes 9437188
  4.4 1.2 %copy-start.2 = (f32[16,64,256]{2,1,0:T(8,128)S(1)}, f32[16,64,256]{2,1,0:T(8,128)}, u32[]{:S(2)}) copy-start(f32[16,64,256]{2,1,0:T(8,128)} %misfit.1) | copy-start | bytes 3145732
  5.6 1.2 %copy-start.3 = (bf16[256,2048]{1,0:T(8,128)(2,1)S(1)}, bf16[256,2048]{1,0:T(8,128)(2,1)}, u32[]{:S(2)}) copy-start(bf16[256,2048]{1,0:T(8,128)(2,1)} %lon_corr.1) | copy-start | bytes 3145732
  6.9 1.0 %copy-start.4 = (bf16[15,64,256]{2,1,0:T(8,128)(2,1)S(1)}, bf16[15,64,256]{2,1,0:T(8,128)(2,1)}, u32[]{:S(2)}) copy-start(bf16[15,64,256]{2,1,0:T(8,128)(2,1)} %mixing.1) | copy-start | bytes 1474564
  7.9 0.8 copy-start.5

commit v2 on v1

--- a/solution.py
+++ b/solution.py
@@ -11,6 +11,7 @@
 BF16 = jnp.bfloat16
 CHUNK = 16
 LANES = 128
+UNROLL = 5
 SUB = 8
 TO_WEST, TO_EAST, TO_SOUTH, TO_NORTH, WIND_EAST, WIND_NORTH = 0, 2, 4, 5, 6, 8
 KINDS = 9
@@ -27,7 +28,8 @@
     lat_corr,
     flux_out,
     state_out,
-    state,
+    state_a,
+    state_b,
     grad,
     send_w,
     send_e,
@@ -49,6 +51,7 @@
     lon_recv,
     lat_send,
     lat_recv,
+    wind_row,
 ):
     steps = east.shape[0]
     levels, rows, cols = misfit.shape
@@ -96,17 +99,19 @@
     def wind_north(k):
         return copy(wind_n.at[k], wind_s.at[k], k, WIND_NORTH, north_id)
 
-    def packed(pack, column, level, place):
+    def packed(pack, tiles, column, level, place):
         for j in range(CHUNK // SUB):
-            tile = jnp.broadcast_to(column[j * SUB : (j + 1) * SUB], (SUB, LANES))
-            pack = jnp.where(lane == level * per + place * (CHUNK // SUB) + j, tile, pack)
+            index = level * per + place * (CHUNK // SUB) + j
+            tile = tiles[j * SUB : (j + 1) * SUB]
+            tile = pltpu.roll(tile, lax.rem(index - column + LANES, LANES), 1)
+            pack = jnp.where(lane == index, tile, pack)
         return pack
 
-    def unpacked(pack, level, place):
+    def unpacked(pack, column, level, place):
         base = level * per + place * (CHUNK // SUB)
         return jnp.concatenate(
             [
-                jnp.broadcast_to(pack[:, base + j : base + j + 1], (SUB, LANES))
+                pltpu.roll(pack, lax.rem(column - base - j + LANES, LANES), 1)
                 for j in range(CHUNK // SUB)
             ],
             axis=0,
@@ -119,7 +124,7 @@
             for place, c in enumerate(members):
                 for level in range(levels):
                     tile = east[n, level, c * CHUNK : (c + 1) * CHUNK, cols - LANES :]
-                    pack = packed(pack, tile.astype(F32)[:, LANES - 1 :], level, place)
+                    pack = packed(pack, tile.astype(F32), LANES - 1, level, place)
             wind_e[k, g] = pack
         edge = [
             north[n, level, rows - CHUNK :, :].astype(F32)[CHUNK - 1 :] for level in range(levels)
@@ -131,16 +136,16 @@
         wind_east(k, 1).start()
         wind_north(k).start()
 
-    state[0] = misfit[...]
+    state_a[...] = misfit[...]
     for g, members in enumerate(groups):
         pack_w = jnp.zeros((SUB, LANES), F32)
         pack_e = jnp.zeros((SUB, LANES), F32)
         for place, c in enumerate(members):
             for level in range(levels):
                 part = slice(c * CHUNK, (c + 1) * CHUNK)
-                pack_w = packed(pack_w, misfit[level, part, :LANES][:, :1], level, place)
+                pack_w = packed(pack_w, misfit[level, part, :LANES], 0, level, place)
                 pack_e = packed(
-                    pack_e, misfit[level, part, cols - LANES :][:, LANES - 1 :], level, place
+                    pack_e, misfit[level, part, cols - LANES :], LANES - 1, level, place
                 )
         send_w[0, g] = pack_w
         send_e[0, g] = pack_e
@@ -175,76 +180,94 @@
             to_north(0).start()
             send_winds(0)
 
-    def work(k, g):
+    def work(k, g, cur, new):
         n = steps - 1 - k
-        cur = lax.rem(k, 2)
-        new = 1 - cur
         halo_e = recv_e[k, g]
         west_term = jnp.minimum(wind_w[k, g], 0.0) * (send_w[k, g] - recv_w[k, g])
         pack_w = jnp.zeros((SUB, LANES), F32)
         pack_e = jnp.zeros((SUB, LANES), F32)
         if g == 0:
-            wind_row = wind_s[k].astype(F32) * keep_south
-        for place, c in enumerate(groups[g]):
+            wind_row[...] = wind_s[k].astype(F32) * keep_south
+        later = jnp.minimum(k + 1, steps)
+
+        def moved(level, place, c):
             r = c * CHUNK
             part = slice(r, r + CHUNK)
-
-            def finish(level, value, pack_w, pack_e):
-                state[new, level, part, :] = value
-                if level == 0:
-                    grad[part, :] += value
-                pack_w = packed(pack_w, value[:, :1], level, place)
-                pack_e = packed(pack_e, value[:, cols - 1 :], level, place)
-                later = jnp.minimum(k + 1, steps)
-                if c == 0:
-                    send_s[later, level : level + 1, :] = value[0:1, :]
-                if c == chunks - 1:
-                    send_n[later, level : level + 1, :] = value[CHUNK - 1 :, :]
-                return pack_w, pack_e
-
-            before = flux = None
-            for level in range(levels):
-                adj = state[cur, level, part, :]
-                ue = east[n, level, part, :].astype(F32)
-                vn = north[n, level, part, :].astype(F32)
-                ahead = pltpu.roll(adj, cols - 1, 1)
-                right = jnp.where(
-                    lane2 == LANES - 1, unpacked(halo_e, level, place), ahead[:, cols - LANES :]
-                )
-                d = jnp.concatenate([ahead[:, : cols - LANES], right], axis=1) - adj
-                back = pltpu.roll(jnp.minimum(ue, 0.0) * d, 1, 1)
-                left = jnp.where(lane2 == 0, unpacked(west_term, level, place), back[:, :LANES])
-                back = jnp.concatenate([left, back[:, LANES:]], axis=1)
-                a = adj + jnp.maximum(ue, 0.0) * d + back
-                if c == chunks - 1:
-                    vn = jnp.where(jnp.logical_and(row2 == CHUNK - 1, top), 0.0, vn)
-                    above = recv_n[k, level : level + 1, :]
-                else:
-                    above = state[cur, level, r + CHUNK : r + CHUNK + 1, :]
-                d = jnp.where(row2 == CHUNK - 1, above, pltpu.roll(adj, CHUNK - 1, 0)) - adj
-                if c == 0:
-                    below = recv_s[k, level : level + 1, :]
-                    vs = wind_row[level : level + 1, :]
-                else:
-                    below = state[cur, level, r - 1 : r, :]
-                    vs = north[n, level, r - CHUNK : r, :].astype(F32)[CHUNK - 1 :]
-                edge = jnp.minimum(vs, 0.0) * (adj[0:1] - below)
-                a = a + jnp.maximum(vn, 0.0) * d
-                a = a + jnp.where(row2 == 0, edge, pltpu.roll(jnp.minimum(vn, 0.0) * d, 1, 0))
-                if level > 0:
-                    flow = mixing[level - 1, part, :].astype(F32) * (a - before)
-                    value = before + flow
-                    if flux is not None:
-                        value = value - flux
-                    pack_w, pack_e = finish(level - 1, value, pack_w, pack_e)
-                    flux = flow
-                before = a
-            pack_w, pack_e = finish(levels - 1, before - flux, pack_w, pack_e)
-        later = jnp.minimum(k + 1, steps)
+            adj = cur[level, part, :]
+            ue = east[n, level, part, :].astype(F32)
+            vn = north[n, level, part, :].astype(F32)
+            ahead = pltpu.roll(adj, cols - 1, 1)
+            right = jnp.where(
+                lane2 == LANES - 1, unpacked(halo_e, LANES - 1, level, place), ahead[:, cols - LANES :]
+            )
+            d = jnp.concatenate([ahead[:, : cols - LANES], right], axis=1) - adj
+            back = pltpu.roll(jnp.minimum(ue, 0.0) * d, 1, 1)
+            left = jnp.where(lane2 == 0, unpacked(west_term, 0, level, place), back[:, :LANES])
+            back = jnp.concatenate([left, back[:, LANES:]], axis=1)
+            a = adj + jnp.maximum(ue, 0.0) * d + back
+            if c == chunks - 1:
+                vn = jnp.where(jnp.logical_and(row2 == CHUNK - 1, top), 0.0, vn)
+                above = recv_n[k, pl.ds(level, 1), :]
+            else:
+                above = cur[level, r + CHUNK : r + CHUNK + 1, :]
+            d = jnp.where(row2 == CHUNK - 1, above, pltpu.roll(adj, CHUNK - 1, 0)) - adj
+            if c == 0:
+                below = recv_s[k, pl.ds(level, 1), :]
+                vs = wind_row[pl.ds(level, 1), :]
+            else:
+                below = cur[level, r - 1 : r, :]
+                vs = north[n, level, r - CHUNK : r, :].astype(F32)[CHUNK - 1 :]
+            edge = jnp.minimum(vs, 0.0) * (adj[0:1] - below)
+            a = a + jnp.maximum(vn, 0.0) * d
+            a = a + jnp.where(row2 == 0, edge, pltpu.roll(jnp.minimum(vn, 0.0) * d, 1, 0))
+            return a
+
+        def finish(level, place, c, value, pack_w, pack_e):
+            new[level, c * CHUNK : (c + 1) * CHUNK, :] = value
+            pack_w = packed(pack_w, value[:, :LANES], 0, level, place)
+            pack_e = packed(pack_e, value[:, cols - LANES :], LANES - 1, level, place)
+            if c == 0:
+                send_s[later, pl.ds(level, 1), :] = value[0:1, :]
+            if c == chunks - 1:
+                send_n[later, pl.ds(level, 1), :] = value[CHUNK - 1 :, :]
+            return pack_w, pack_e
+
+        def climb(level, carry):
+            before, flux, pack_w, pack_e = carry
+            above, flows = [], []
+            for place, c in enumerate(groups[g]):
+                a = moved(level, place, c)
+                kappa = mixing[level - 1, c * CHUNK : (c + 1) * CHUNK, :].astype(F32)
+                flow = kappa * (a - before[place])
+                value = before[place] + flow - flux[place]
+                pack_w, pack_e = finish(level - 1, place, c, value, pack_w, pack_e)
+                above.append(a)
+                flows.append(flow)
+            return tuple(above), tuple(flows), pack_w, pack_e
+
+        def climb_some(i, carry):
+            for u in range(UNROLL):
+                carry = climb(1 + i * UNROLL + u, carry)
+            return carry
+
+        members = groups[g]
+        first = tuple(moved(0, place, c) for place, c in enumerate(members))
+        nothing = tuple(jnp.zeros((CHUNK, cols), F32) for _ in members)
+        turns = (levels - 1) // UNROLL
+        carry = lax.fori_loop(0, turns, climb_some, (first, nothing, pack_w, pack_e))
+        for level in range(1 + turns * UNROLL, levels):
+            carry = climb(level, carry)
+        before, flux, pack_w, pack_e = carry
+        for place, c in enumerate(members):
+            pack_w, pack_e = finish(
+                levels - 1, place, c, before[place] - flux[place], pack_w, pack_e
+            )
+            part = slice(c * CHUNK, (c + 1) * CHUNK)
+            grad[part, :] += new[0, part, :]
         send_w[later, g] = pack_w
         send_e[later, g] = pack_e
 
-    def step(k, carry):
+    def step(k, cur, new):
         @pl.when(k + 1 < steps)
         def _():
             pack_winds(k + 1)
@@ -256,7 +279,7 @@
         to_north(k).wait_recv()
         wind_east(k, 0).wait_recv()
         wind_north(k).wait_recv()
-        work(k, 0)
+        work(k, 0, cur, new)
 
         @pl.when(k + 1 < steps)
         def _():
@@ -268,16 +291,23 @@
         to_west(k, 1).wait_recv()
         to_east(k, 1).wait_recv()
         wind_east(k, 1).wait_recv()
-        work(k, 1)
+        work(k, 1, cur, new)
 
         @pl.when(k + 1 < steps)
         def _():
             to_west(k + 1, 1).start()
             to_east(k + 1, 1).start()
 
+    def pair(i, carry):
+        step(2 * i, state_a, state_b)
+        step(2 * i + 1, state_b, state_a)
         return carry
 
-    lax.fori_loop(0, steps, step, 0)
+    lax.fori_loop(0, steps // 2, pair, 0)
+    last = state_a
+    if steps % 2:
+        step(steps - 1, state_a, state_b)
+        last = state_b
 
     band[lon] = (grad[...] / steps).astype(BF16)
 
@@ -302,7 +332,7 @@
         )
 
     total = product(0)
-    state_out[...] = state[steps % 2]
+    state_out[...] = last[...]
     for d in range(1, n_lon):
         spread(d).wait_recv()
         total = total + product(d)
@@ -361,7 +391,8 @@
         in_specs=[vmem] * 6,
         out_specs=(vmem, vmem),
         scratch_shapes=[
-            pltpu.VMEM((2, levels, rows, cols), F32),
+            pltpu.VMEM((levels, rows, cols), F32),
+            pltpu.VMEM((levels, rows, cols), F32),
             pltpu.VMEM((rows, cols), F32),
             pltpu.VMEM(pack_out, F32),
             pltpu.VMEM(pack_out, F32),
@@ -383,6 +414,7 @@
             dma((n_lon,)),
             dma((n_lat,)),
             dma((n_lat,)),
+            pltpu.VMEM((levels, cols), F32),
         ],
         compiler_params=pltpu.CompilerParams(
             collective_id=0, has_side_effects=True, vmem_limit_bytes=40 * 1024 * 1024

time: 77 us -> 58 us (0.75)
  Pallas kernels: 66.3 us -> 47.4 us
    pallas_call x1, Pallas kernels: 66.3 us -> 47.4 us  [per_device(): pl.pallas_call(functools.partial(kernel, n_lon, n_lat), out_shape=(jax.Sh...]
where the time goes in v2:
time: 58 us; the launch traced here: 57.6 us
  Pallas kernels  47.4 us (82%)
  local copies, waits for them, and re-layouts  9.61 us (17%)
  between operations  0.65 us (1%)
    pallas_call x1, Pallas kernels, per_device(): pl.pallas_call(functools.partial(kernel, n_lon, n_lat), out_shape=(jax.Sh...  47.4 us
    unnamed x14, local copies, waits for them, and re-layouts  9.61 us

profile of v2, /device:TPU:0, one launch (start us, length us, event | category | flops | bytes accessed | tf_op | source)
XLA Modules:
  0.0 57.6 jit_solution(13400302904112927220)
XLA Ops:
  0.6 0.0 copy-start
  0.6 1.9 %copy-done = bf16[6,16,64,256]{3,2,1,0:T(8,128)(2,1)S(1)} copy-done((bf16[6,16,64,256]{3,2,1,0:T(8,128)(2,1)S(1)}, bf16[6,16,64,256]{3,2,1,0:T(8,128)(2,1)}, u32[]{:S(2)}) %copy-start) | copy-done | bytes 3145752
  2.5 0.0 copy-start.1
  2.5 1.9 %copy-done.1 = bf16[6,16,64,256]{3,2,1,0:T(8,128)(2,1)S(1)} copy-done((bf16[6,16,64,256]{3,2,1,0:T(8,128)(2,1)S(1)}, bf16[6,16,64,256]{3,2,1,0:T(8,128)(2,1)}, u32[]{:S(2)}) %copy-start.1) | copy-done | bytes 3145752
  4.4 0.0 copy-start.2
  4.4 1.2 %copy-done.2 = f32[16,64,256]{2,1,0:T(8,128)S(1)} copy-done((f32[16,64,256]{2,1,0:T(8,128)S(1)}, f32[16,64,256]{2,1,0:T(8,128)}, u32[]{:S(2)}) %copy-start.2) | copy-done | bytes 1048600
  5.6 0.0 copy-start.3
  5.6 1.2 %copy-done.3 = bf16[256,2048]{1,0:T(8,128)(2,1)S(1)} copy-done((bf16[256,2048]{1,0:T(8,128)(2,1)S(1)}, bf16[256,2048]{1,0:T(8,128)(2,1)}, u32[]{:S(2)}) %copy-start.3) | copy-done | bytes 1048600
  6.9 0.0 copy-start.4
  6.9 1.0 %copy-done.4 = bf16[15,64,256]{2,1,0:T(8,128)(2,1)S(1)} copy-done((bf16[15,64,256]{2,1,0:T(8,128)(2,1)S(1)}, bf16[15,64,256]{2,1,0:T(8,128)(2,1)}, u32[]{:S(2)}) %copy-start.4) | copy-done | bytes 491544
  7.9 0.0 copy-start.5
  7.9 0.8 %copy-done.5 = bf16[64,256]{1,0:T(8,128)(2,1)S(1)} copy-done((bf16[64,256]{1,0:T(8,128)(2,1)S(1)}, bf16[64,256]{1,0:T(8,128)(2,1)}, u32[]{:S(2)}) %copy-start.5) | copy-done | bytes 32792
  8.7 47.4 %shard_map.77 = (f32[64,256]{1,0:T(8,128)S(1)}, f32[16,64,256]{2,1,0:T(8,128)S(1)}) custom-call(f32[16,64,256]{2,1,0:T(8,128)S(1)} %copy-done.2, bf16[6,16,64,256]{3,2,1,0:T(8,128)(2,1)S(1)} %copy-done, bf16[6,16,64,256]{3,2,1,0:T(8,128)(2,1)S(1)} %copy-done.1, bf16[15,64,256]{2,1,0:T(8,128)(2,1)S(1)} %copy-done.4, bf16[256,2048]{1,0:T(8,128)(2,1)S(1)} %copy-done.3, ...), custom_call_target="tpu_custom_call" | custom-call | tf_op jit(solution)/shard_map/pallas_call | solution.py:385
  56.0 0.6 %copy.10 = f32[64,256]{1,0:T(8,128)} copy(f32[64,256]{1,0:T(8,128)S(1)} %get-tuple-element.4) | data formatting | bytes 131072
  56.6 1.0 %copy.11 = f32[16,64,256]{2,1,0:T(8,128)} copy(f32[16,64,256]{2,1,0:T(8,128)S(1)} %get-tuple-element.5) | data formatting | bytes 2097152
Async XLA Ops:
  0.6 1.9 %copy-start = (bf16[6,16,64,256]{3,2,1,0:T(8,128)(2,1)S(1)}, bf16[6,16,64,256]{3,2,1,0:T(8,128)(2,1)}, u32[]{:S(2)}) copy-start(bf16[6,16,64,256]{3,2,1,0:T(8,128)(2,1)} %east.1) | copy-start | bytes 9437188
  2.5 1.9 %copy-start.1 = (bf16[6,16,64,256]{3,2,1,0:T(8,128)(2,1)S(1)}, bf16[6,16,64,256]{3,2,1,0:T(8,128)(2,1)}, u32[]{:S(2)}) copy-start(bf16[6,16,64,256]{3,2,1,0:T(8,128)(2,1)} %north.1) | copy-start | bytes 9437188
  4.4 1.2 %copy-start.2 = (f32[16,64,256]{2,1,0:T(8,128)S(1)}, f32[16,64,256]{2,1,0:T(8,128)}, u32[]{:S(2)}) copy-start(f32[16,64,256]{2,1,0:T(8,128)} %misfit.1) | copy-start | bytes 3145732
  5.6 1.2 %copy-start.3 = (bf16[256,2048]{1,0:T(8,128)(2,1)S(1)}, bf16[256,2048]{1,0:T(8,128)(2,1)}, u32[]{:S(2)}) copy-start(bf16[256,2048]{1,0:T(8,128)(2,1)} %lon_corr.1) | copy-start | bytes 3145732
  6.9 1.0 %copy-start.4 = (bf16[15,64,256]{2,1,0:T(8,128)(2,1)S(1)}, bf16[15,64,256]{2,1,0:T(8,128)(2,1)}, u32[]{:S(2)}) copy-start(bf16[15,64,256]{2,1,0:T(8,128)(2,1)} %mixing.1) | copy-start | bytes 1474564
  7.9 0.8 %copy-start.5 = (bf16[64,256]{1,0:T(8,128)(2,1)S(1)}, bf16[64,256]{1,0:T(8,128)(2,1)}, u32[]{:S(2)}) copy-start(bf16[64,256]{1,0:T(8,128)(2,1)} %lat_corr.1) | copy-start | bytes 98308

commit v3 on v2

--- a/solution.py
+++ b/solution.py
@@ -20,12 +20,12 @@
 def kernel(
     n_lon,
     n_lat,
-    misfit,
-    east,
-    north,
-    mixing,
-    lon_corr,
-    lat_corr,
+    misfit_in,
+    east_in,
+    north_in,
+    mixing_in,
+    lon_in,
+    lat_in,
     flux_out,
     state_out,
     state_a,
@@ -52,10 +52,34 @@
     lat_send,
     lat_recv,
     wind_row,
+    east,
+    north,
+    mixing,
+    lon_corr,
+    lat_corr,
+    wind_sem,
+    in_sem,
 ):
     steps = east.shape[0]
-    levels, rows, cols = misfit.shape
+    levels, rows, cols = state_a.shape
     chunks = rows // CHUNK
+
+    def fetched(i):
+        source, target = (
+            (misfit_in, state_a),
+            (mixing_in, mixing),
+            (lon_in, lon_corr),
+            (lat_in, lat_corr),
+        )[i]
+        return pltpu.make_async_copy(source, target, in_sem.at[i])
+
+    def fetched_wind(n, i):
+        source, target = ((east_in, east), (north_in, north))[i]
+        return pltpu.make_async_copy(source.at[n], target.at[n], wind_sem.at[n, i])
+
+    fetched(0).start()
+    for i in range(2):
+        fetched_wind(steps - 1, i).start()
     per = chunks // 2 * (CHUNK // SUB)
     order = (0, chunks - 1) + tuple(range(1, chunks - 1))
     groups = (order[: chunks // 2], order[chunks // 2 :])
@@ -119,6 +143,8 @@
 
     def pack_winds(k):
         n = steps - 1 - k
+        fetched_wind(n, 0).wait()
+        fetched_wind(n, 1).wait()
         for g, members in enumerate(groups):
             pack = jnp.zeros((SUB, LANES), F32)
             for place, c in enumerate(members):
@@ -136,22 +162,22 @@
         wind_east(k, 1).start()
         wind_north(k).start()
 
-    state_a[...] = misfit[...]
+    fetched(0).wait()
     for g, members in enumerate(groups):
         pack_w = jnp.zeros((SUB, LANES), F32)
         pack_e = jnp.zeros((SUB, LANES), F32)
         for place, c in enumerate(members):
             for level in range(levels):
                 part = slice(c * CHUNK, (c + 1) * CHUNK)
-                pack_w = packed(pack_w, misfit[level, part, :LANES], 0, level, place)
+                pack_w = packed(pack_w, state_a[level, part, :LANES], 0, level, place)
                 pack_e = packed(
-                    pack_e, misfit[level, part, cols - LANES :], LANES - 1, level, place
+                    pack_e, state_a[level, part, cols - LANES :], LANES - 1, level, place
                 )
         send_w[0, g] = pack_w
         send_e[0, g] = pack_e
     for level in range(levels):
-        send_s[0, level : level + 1, :] = misfit[level, 0:1, :]
-        send_n[0, level : level + 1, :] = misfit[level, rows - 1 : rows, :]
+        send_s[0, level : level + 1, :] = state_a[level, 0:1, :]
+        send_n[0, level : level + 1, :] = state_a[level, rows - 1 : rows, :]
     pack_winds(0)
     grad[...] = jnp.zeros_like(grad)
 
@@ -179,6 +205,14 @@
             to_south(0).start()
             to_north(0).start()
             send_winds(0)
+
+    fetched(1).start()
+    for k in range(1, min(2, steps)):
+        for i in range(2):
+            fetched_wind(steps - 1 - k, i).start()
+    fetched(2).start()
+    fetched(3).start()
+    fetched(1).wait()
 
     def work(k, g, cur, new):
         n = steps - 1 - k
@@ -273,6 +307,11 @@
             pack_winds(k + 1)
             send_winds(k + 1)
 
+        @pl.when(k + 2 < steps)
+        def _():
+            fetched_wind(steps - 3 - k, 0).start()
+            fetched_wind(steps - 3 - k, 1).start()
+
         to_west(k, 0).wait_recv()
         to_east(k, 0).wait_recv()
         to_south(k).wait_recv()
@@ -331,6 +370,8 @@
             band[src], block, (((1,), (1,)), ((), ())), preferred_element_type=F32
         )
 
+    fetched(2).wait()
+    fetched(3).wait()
     total = product(0)
     state_out[...] = last[...]
     for d in range(1, n_lon):
@@ -388,7 +429,7 @@
             jax.ShapeDtypeStruct((rows, cols), F32),
             jax.ShapeDtypeStruct(misfit.shape, F32),
         ),
-        in_specs=[vmem] * 6,
+        in_specs=[pl.BlockSpec(memory_space=pltpu.HBM)] * 6,
         out_specs=(vmem, vmem),
         scratch_shapes=[
             pltpu.VMEM((levels, rows, cols), F32),
@@ -415,9 +456,16 @@
             dma((n_lat,)),
             dma((n_lat,)),
             pltpu.VMEM((levels, cols), F32),
+            pltpu.VMEM(east_wind.shape, BF16),
+            pltpu.VMEM(north_wind.shape, BF16),
+            pltpu.VMEM(mixing.shape, BF16),
+            pltpu.VMEM(lon_corr.shape, BF16),
+            pltpu.VMEM(lat_corr.shape, BF16),
+            dma((steps, 2)),
+            dma((4,)),
         ],
         compiler_params=pltpu.CompilerParams(
-            collective_id=0, has_side_effects=True, vmem_limit_bytes=40 * 1024 * 1024
+            collective_id=0, has_side_effects=True, vmem_limit_bytes=63 * 1024 * 1024
         ),
     )(misfit, east_wind, north_wind, mixing, lon_corr, lat_corr)
 

time: 58 us -> 54.6 us (0.941)
  local copies, waits for them, and re-layouts: 9.61 us -> 3.77 us
  Pallas kernels: 47.4 us -> 50 us
    unnamed x14 -> x2, local copies, waits for them, and re-layouts: 9.61 us -> 3.77 us
    pallas_call x1, Pallas kernels: 47.4 us -> 50 us  [per_device(): pl.pallas_call(functools.partial(kernel, n_lon, n_lat), out_shape=(jax.Sh...]
where the time goes in v3:
time: 54.6 us; the launch traced here: 54.4 us
  Pallas kernels  50 us (92%)
  local copies, waits for them, and re-layouts  3.77 us (7%)
  between operations  0.64 us (1%)
    pallas_call x1, Pallas kernels, per_device(): pl.pallas_call(functools.partial(kernel, n_lon, n_lat), out_shape=(jax.Sh...  50 us
    unnamed x2, local copies, waits for them, and re-layouts  3.77 us

profile of v3, /device:TPU:0, one launch (start us, length us, event | category | flops | bytes accessed | tf_op | source)
XLA Modules:
  0.0 54.4 jit_solution(10447840516010764217)
XLA Ops:
  0.6 50.0 %shard_map.77 = (f32[64,256]{1,0:T(8,128)}, f32[16,64,256]{2,1,0:T(8,128)}) custom-call(f32[16,64,256]{2,1,0:T(8,128)} %misfit_in.1, bf16[6,16,64,256]{3,2,1,0:T(8,128)(2,1)} %east_in.1, bf16[6,16,64,256]{3,2,1,0:T(8,128)(2,1)} %north_in.1, bf16[15,64,256]{2,1,0:T(8,128)(2,1)} %mixing_in.1, bf16[256,2048]{1,0:T(8,128)(2,1)} %lon_in.1, bf16[64,256]{1,0:T(8,128)(2,1)} %lat_in.1), custom_call_target="tpu_custom_call" | custom-call | tf_op jit(solution)/shard_map/pallas_call | solution.py:426
  50.6 1.5 %copy.10 = f32[64,256]{1,0:T(8,128)} copy(f32[64,256]{1,0:T(8,128)} %get-tuple-element.4) | data formatting | bytes 131072
  52.1 2.3 %copy.11 = f32[16,64,256]{2,1,0:T(8,128)} copy(f32[16,64,256]{2,1,0:T(8,128)} %get-tuple-element.5) | data formatting | bytes 2097152
